TPU v7x, 128 devices: a whole 4x4x4 slice. The times are simulated.
128 devices in a mesh: occ: 8 (over z_hi, x), vir: 16 (over z_lo, y, core).
Axes of the slice: x: 4, y: 4, z: 4 (z_hi: 2, z_lo: 2; z = z_hi * 2 + z_lo), core: 2. Of those that a mesh axis runs over, the one named last changes fastest.
Arguments:
- amplitudes: bfloat16 [4096, 32, 2048], P(('occ', 'vir')), may hold values from -6 to 6
- cycle_inter: bfloat16 [2048, 2048], P(None, ('occ', 'vir')), may hold values from -0.125 to 0.125
- ladder_slab: bfloat16 [32, 256, 2048], P(None, None, 'vir'), may hold values from -0.0625 to 0.0625
- irrep_counts: int32 [8], replicated, may hold values from 144 to 256, as said below
- slab_irrep: int32 [1], replicated, may hold values from 1 to 7
Outputs:
- ladder: bfloat16 [4096, 2048], P('occ', 'vir')
Inputs may be any that keep to these rules, and one draw needn't show every extreme that they name: `irrep_counts`: the counts sum to 1600.
All inputs are finite; a program needn't handle non-finite values.
Results may differ from a plain program's by a relative error of at most 0.0049.
Values may be sent and summed in bfloat16 or wider, within the bound.
A program may use at most 128 MiB of HBM per device.

v0:
```python
import jax
import jax.numpy as jnp
from jax import lax
from jax.sharding import PartitionSpec as P

BLK = 256


def from_partner(array, axis, distance):
    return lax.ppermute(array, axis, [(i, i ^ 1 << distance) for i in range(lax.axis_size(axis))])


def live_columns(irrep_counts, first_col, col_count):
    col_index = first_col + jnp.arange(col_count, dtype=jnp.int32)
    block_of = col_index // BLK
    matches = block_of[:, None] == jnp.arange(8, dtype=jnp.int32)[None, :]
    live_bound = jnp.sum(jnp.where(matches, irrep_counts[None, :], 0), axis=1)
    return (col_index % BLK < live_bound).astype(jnp.float32)


def body(amplitudes, cycle_inter, ladder_slab, irrep_counts, slab_irrep):
    pair_count, window, padded = amplitudes.shape
    live_all = live_columns(irrep_counts, 0, padded)
    masked = jnp.where(live_all > 0, amplitudes, jnp.zeros_like(amplitudes))
    flattened = masked.reshape(pair_count * window, padded)
    columns = lax.all_gather(cycle_inter, ("occ", "vir"), axis=1, tiled=True)
    col_count = columns.shape[1]
    own_part = flattened.astype(jnp.float32)
    dressed_part = own_part + jnp.dot(flattened, columns, preferred_element_type=jnp.float32)
    dressed = (dressed_part * live_columns(irrep_counts, jnp.int32(0), col_count)).astype(
        jnp.bfloat16
    )
    dressed_cube = dressed.reshape(pair_count, window, padded)
    slab_index = slab_irrep[0]
    group_size = lax.axis_size("vir") // 8
    low_bits = group_size.bit_length() - 1
    position = lax.axis_index("vir")
    owned = lax.all_to_all(dressed_cube, "vir", split_axis=2, concat_axis=0, tiled=True)
    for bit_number in range(3):
        partner = from_partner(owned, "vir", bit_number + low_bits)
        take_flag = jnp.bitwise_and(jnp.right_shift(slab_index, bit_number), 1)
        owned = jnp.where(take_flag == 1, partner, owned)
    row_count = owned.shape[0]
    own_cols = ladder_slab.shape[2]
    full_block = owned
    bit_number = 0
    neighbor = from_partner(full_block, "vir", bit_number)
    low_side = jnp.bitwise_and(jnp.right_shift(position, bit_number), 1) == 0
    leading = jnp.where(low_side, full_block, neighbor)
    trailing = jnp.where(low_side, neighbor, full_block)
    full_block = jnp.concatenate([leading, trailing], axis=2)
    result = jnp.dot(
        full_block.reshape(row_count, window * BLK),
        ladder_slab.reshape(window * BLK, own_cols),
        preferred_element_type=jnp.float32,
    )
    live_own = live_columns(irrep_counts, position * own_cols, own_cols)
    return (result * live_own).astype(jnp.bfloat16)


def solution(mesh):
    placed = (
        P(("occ", "vir"), None, None),
        P(None, ("occ", "vir")),
        P(None, None, "vir"),
        P(),
        P(),
    )
    return jax.shard_map(
        body, mesh=mesh, in_specs=placed, out_specs=P("occ", "vir"), check_vma=False
    )
```

profile of v0, /device:TPU:1, one launch (start us, length us, event | category | flops | bytes accessed | tf_op | source)
XLA Modules:
  0.0 671.9 jit_solution(8007329297174539401)
XLA Ops:
  6.5 0.0 copy-start
  6.5 0.0 all-gather.2.cloned.1.call-start
  6.5 0.7 all-gather.2.cloned.1.call-update
  7.3 0.7 select_reduce_fusion
  8.0 4.4 broadcast_select_fusion
  12.4 202.7 %all-gather.2.cloned.1.call-done = bf16[2048,2048]{0,1:T(8,128)(2,1)} async-done(((bf16[2048,16]{0,1:T(8,128)(2,1)}), bf16[2048,2048]{0,1:T(8,128)(2,1)}) %all-gather.2.cloned.1.call-update) | async-done | bytes 8388624 | tf_op jit(solution)/shard_map/all_gather | solution.py:26
  215.2 14.5 %multiply_convert_fusion = bf16[1024,2048]{1,0:T(8,128)(2,1)} fusion(bf16[1024,2048]{1,0:T(8,128)(2,1)} %bitcast.25, f32[2048]{0:T(1024)S(1)} %get-tuple-element.7, bf16[2048,2048]{0,1:T(8,128)(2,1)} %all-gather.2.cloned.1.call-done), kind=kOutput, calls=%fused_computation.4 | convolution fusion | flops 8598323200 | bytes 16785408 | tf_op jit(solution)/shard_map/dot_general | solution.py:29
  229.7 23.0 %copy.9 = bf16[32,32,2048]{1,0,2:T(8,128)(2,1)} copy(bf16[32,32,2048]{2,1,0:T(8,128)(2,1)} %bitcast.24) | data formatting | bytes 8388608 | tf_op jit(solution)/shard_map/reshape | solution.py:33
  252.7 20.7 %reshape.94 = bf16[16,2,65536]{2,1,0:T(2,128)(2,1)} reshape(bf16[2048,32,32]{2,1,0:T(8,128)(2,1)} %bitcast.21) | data formatting | bytes 8388608
  273.4 54.8 %all_to_all.18 = bf16[16,2,65536]{2,1,0:T(2,128)(2,1)} all-to-all(bf16[16,2,65536]{2,1,0:T(2,128)(2,1)} %reshape.94), channel_id=1, replica_groups=mesh['occ'=8,'vir'=16] {'vir'}, dimensions={0} | all-to-all | bytes 8388608 | tf_op jit(solution)/shard_map/all_to_all | solution.py:38
  328.2 16.0 %reshape.95 = bf16[2048,32,32]{2,1,0:T(8,128)(2,1)} reshape(bf16[16,2,65536]{2,1,0:T(2,128)(2,1)} %all_to_all.18) | data formatting | bytes 8388608
  344.2 24.5 %copy.10 = bf16[32,32,16,128]{3,0,2,1:T(8,128)(2,1)} copy(bf16[32,32,16,128]{1,0,3,2:T(8,128)(2,1)} %bitcast.22) | data formatting | bytes 8388608 | tf_op jit(solution)/shard_map/all_to_all | solution.py:38
  368.7 0.0 collective-permute-start
  369.3 90.6 %collective-permute-done = bf16[512,32,128]{2,0,1:T(8,128)(2,1)S(1)} collective-permute-done((bf16[512,32,128]{2,0,1:T(8,128)(2,1)}, bf16[512,32,128]{2,0,1:T(8,128)(2,1)S(1)}, u32[]{:S(2)}, u32[]{:S(2)}) %collective-permute-start) | collective-permute-done | bytes 4194336 | tf_op jit(solution)/shard_map/ppermute | solution.py:10
  459.9 2.6 broadcast_select_fusion.1
  462.5 2.3 collective-permute-start.1
  464.8 89.4 %collective-permute-done.1 = bf16[512,32,128]{2,0,1:T(8,128)(2,1)S(1)} collective-permute-done((bf16[512,32,128]{2,0,1:T(8,128)(2,1)S(1)}, bf16[512,32,128]{2,0,1:T(8,128)(2,1)S(1)}, u32[]{:S(2)}, u32[]{:S(2)}) %collective-permute-start.1) | collective-permute-done | bytes 4194336 | tf_op jit(solution)/shard_map/ppermute | solution.py:10
  554.2 0.4 broadcast_select_fusion.2
  554.6 2.4 collective-permute-start.2
  557.1 88.6 %collective-permute-done.2 = bf16[512,32,128]{2,0,1:T(8,128)(2,1)S(1)} collective-permute-done((bf16[512,32,128]{2,0,1:T(8,128)(2,1)S(1)}, bf16[512,32,128]{2,0,1:T(8,128)(2,1)S(1)}, u32[]{:S(2)}, u32[]{:S(2)}) %collective-permute-start.2) | collective-permute-done | bytes 4194336 | tf_op jit(solution)/shard_map/ppermute | solution.py:10
  645.6 0.0 copy-start.1
  645.6 2.4 broadcast_select_fusion.3
  648.0 2.9 collective-permute-start.3
  651.0 0.0 copy-done.1
  651.0 0.1 select_reduce_fusion.1
  651.1 7.0 %collective-permute-done.3 = bf16[512,32,128]{2,0,1:T(8,128)(2,1)} collective-permute-done((bf16[512,32,128]{2,0,1:T(8,128)(2,1)}, bf16[512,32,128]{2,0,1:T(8,128)(2,1)}, u32[]{:S(2)}, u32[]{:S(2)}) %collective-permute-start.3) | collective-permute-done | bytes 4194336 | tf_op jit(solution)/shard_map/ppermute | solution.py:10
  658.1 3.8 broadcast_select_fusion.5
  661.8 0.0 copy-done
  661.9 3.2 fusion.10
  (4 shorter events, 0.0 us)
Async XLA Ops:
  6.5 655.3 %copy-start = (bf16[32,256,128]{2,1,0:T(8,128)(2,1)S(1)}, bf16[32,256,128]{2,1,0:T(8,128)(2,1)}, u32[]{:S(2)}) copy-start(bf16[32,256,128]{2,1,0:T(8,128)(2,1)} %param.7) | copy-start | bytes 6291460
  6.5 208.6 %all-gather.2.cloned.1.call-start = ((), (), s32[]{:S(2)}) async-start(), calls=%async_computation.1 | async-start | bytes 8454144 | tf_op jit(solution)/shard_map/all_gather | solution.py:26
  368.7 91.2 %collective-permute-start = (bf16[512,32,128]{2,0,1:T(8,128)(2,1)}, bf16[512,32,128]{2,0,1:T(8,128)(2,1)S(1)}, u32[]{:S(2)}, u32[]{:S(2)}) collective-permute-start(bf16[512,32,128]{2,0,1:T(8,128)(2,1)} %bitcast.23), channel_id=1, source_target_pairs={{0,2},{1,3},{2,0},{3,1},{4,6},{5,7},{6,4},{7,5},{8,10},{9,11},{10,... | collective-permute-start | bytes 12582920 | tf_op jit(solution)/shard_map/ppermute | solution.py:10
  462.5 91.7 %collective-permute-start.1 = (bf16[512,32,128]{2,0,1:T(8,128)(2,1)S(1)}, bf16[512,32,128]{2,0,1:T(8,128)(2,1)S(1)}, u32[]{:S(2)}, u32[]{:S(2)}) collective-permute-start(bf16[512,32,128]{2,0,1:T(8,128)(2,1)S(1)} %broadcast_select_fusion.1), channel_id=1, source_target_pairs={{0,4},{1,5},{2,6},{3,7},{4,0},{5,1},{6,2},{7,3},{8,12},{9,13},{10,... | collective-permute-start | bytes 12582920 | tf_op jit(solution)/shard_map/ppermute | solution.py:10
  554.6 91.0 %collective-permute-start.2 = (bf16[512,32,128]{2,0,1:T(8,128)(2,1)S(1)}, bf16[512,32,128]{2,0,1:T(8,128)(2,1)S(1)}, u32[]{:S(2)}, u32[]{:S(2)}) collective-permute-start(bf16[512,32,128]{2,0,1:T(8,128)(2,1)S(1)} %broadcast_select_fusion.2), channel_id=1, source_target_pairs={{0,8},{1,9},{2,10},{3,11},{4,12},{5,13},{6,14},{7,15},{8,0},{9,1},... | collective-permute-start | bytes 12582920 | tf_op jit(solution)/shard_map/ppermute | solution.py:10
  645.6 5.3 copy-start.1
  648.0 10.1 %collective-permute-start.3 = (bf16[512,32,128]{2,0,1:T(8,128)(2,1)}, bf16[512,32,128]{2,0,1:T(8,128)(2,1)}, u32[]{:S(2)}, u32[]{:S(2)}) collective-permute-start(bf16[512,32,128]{2,0,1:T(8,128)(2,1)} %broadcast_select_fusion.3), channel_id=1, source_target_pairs={{0,1},{1,0},{2,3},{3,2},{4,5},{5,4},{6,7},{7,6},{8,9},{9,8},{10,11... | collective-permute-start | bytes 12582920 | tf_op jit(solution)/shard_map/ppermute | solution.py:10
Sparse Core Ops, SparseCore 0:
  9.1 206.0 all-gather.1
where the time goes:
time: 673 us; the launch traced here: 672 us
  waiting for transfers between devices  479 us (71%)
  local copies, waits for them, and re-layouts  84.2 us (13%)
  blocking collectives  54.8 us (8%)
  matrix products  17.7 us (3%)
  other arithmetic  14.5 us (2%)
  between operations  14.1 us (2%)
  starting transfers between devices  7.63 us (1%)
    ppermute x4, waiting for transfers between devices, from_partner(): lax.ppermute(array, axis, [(i, i ^ 1 << distance) for i in range(lax.axis...  276 us
    all_gather x1, waiting for transfers between devices, body(): columns = lax.all_gather(cycle_inter, ('occ', 'vir'), axis=1, tiled=True)  203 us
    all_to_all x1, blocking collectives, body(): lax.all_to_all(dressed_cube, 'vir', split_axis=2, concat_axis=0, tiled=True)  54.8 us
    unnamed x6, local copies, waits for them, and re-layouts  36.7 us
    all_to_all x1, local copies, waits for them, and re-layouts, body(): lax.all_to_all(dressed_cube, 'vir', split_axis=2, concat_axis=0, tiled=True)  24.5 us
    reshape x1, local copies, waits for them, and re-layouts, body(): dressed_cube = dressed.reshape(pair_count, window, padded)  23 us
    dot_general x1, matrix products, body(): jnp.dot(flattened, columns, preferred_element_type=jnp.float32)  14.5 us
  transfers between devices with their start and end apart: 5, of which 5 were waited for; matrix products, arithmetic and copies ran while one was open for 1% of the time, Pallas kernels for 0%

commit v1 on v0

v1 whole, which is shorter than its diff:
```python
import jax
import jax.numpy as jnp
from jax import lax
from jax.experimental import pallas as pl
from jax.experimental.pallas import tpu as pltpu
from jax.sharding import PartitionSpec as P

BLK = 256
WIDTHS = (768, 640, 640)
ORDERS = ("yzx", "zxy", "xyz")
NR = 4
MESH = pl.DeviceIdType.MESH
F32 = jnp.float32
BF16 = jnp.bfloat16
ALL = slice(None)


def device(x, y, z, core):
    return (z // 2 * 4 + x, z % 2 * 8 + y * 2 + core)


def kernel(
    amp_hbm, cyc_hbm, slab_hbm, counts, table, out_ref,
    raw, trans, amp, g0, g1, g2, dressed, recv, slab, total, mine, theirs,
    local_sem, gather_send, gather_recv, sib_send, sib_recv, a2a_send, a2a_recv, fin_sem,
):
    occ, vir = lax.axis_index("occ"), lax.axis_index("vir")
    x, y, core = occ % 4, vir // 2 % 4, vir % 2
    zh, zl = occ // 4, vir // 8
    z = zh * 2 + zl
    my_h = vir // 2
    gs = (g0, g1, g2)
    pos = {"x": x, "y": y, "z": z}
    sibling = device(x, y, z, 1 - core)

    def neighbour(dim, step):
        at = dict(pos)
        at[dim] = (at[dim] + step) % 4
        return device(at["x"], at["y"], at["z"], core)

    load_amp = pltpu.make_async_copy(amp_hbm, raw, local_sem.at[0])
    load_amp.start()
    half = pl.ds(pl.multiple_of(core * 128, 128), 128)
    load_slab = pltpu.make_async_copy(slab_hbm, slab.at[:, :, half], local_sem.at[1])
    load_slab.start()
    offset = 0
    load_cyc = []
    for p in range(3):
        w = WIDTHS[p]
        load_cyc.append(
            pltpu.make_async_copy(
                cyc_hbm.at[:, pl.ds(offset, w)], gs[p].at[zh, x, zl, y, core], local_sem.at[2 + p]
            )
        )
        load_cyc[-1].start()
        offset += w

    barrier = pltpu.get_barrier_semaphore()
    peers = [((my_h // 4 + j // 4) % 2) * 4 + (my_h + j) % 4 for j in range(8)]
    greet = [sibling, neighbour("x", 1), neighbour("x", 3)]
    outer_z = (z + 3 + 2 * zl) % 4
    greet.append(device(x, y, outer_z, core))
    greet += [(occ, peers[j] * 2 + core) for j in range(1, 8)]
    for who in greet:
        pl.semaphore_signal(barrier, inc=1, device_id=who, device_id_type=MESH)
    pl.semaphore_wait(barrier, len(greet))

    def region(p, phase, k, part):
        done = ORDERS[p][:phase]
        dim = ORDERS[p][phase]
        at = {}
        for name in "xyz":
            at[name] = ALL if name in done else pos[name]
        at[dim] = k
        zhi, zlo = (ALL, ALL) if "z" in done else (at["z"] // 2, at["z"] % 2)
        xs, ys = at["x"], at["y"]
        if part is not None and phase > 0:
            if "z" in done:
                zhi = part
            elif "x" in done:
                xs = pl.ds(2 * part, 2)
            else:
                ys = pl.ds(2 * part, 2)
        return gs[p].at[zhi, xs, zlo, ys, core]

    def piece(p, phase, k, part, slot, who):
        ref = region(p, phase, k, part)
        return pltpu.make_async_remote_copy(
            src_ref=ref, dst_ref=ref,
            send_sem=gather_send.at[p, phase, slot], recv_sem=gather_recv.at[p, phase, slot],
            device_id=who, device_id_type=MESH,
        )

    def to_sibling(p, ref, slot):
        return pltpu.make_async_remote_copy(
            src_ref=ref, dst_ref=ref,
            send_sem=sib_send.at[p, slot], recv_sem=sib_recv.at[p, slot],
            device_id=sibling, device_id_type=MESH,
        )

    def sib_wait(p, ref_of, slot):
        ref = ref_of
        return pltpu.make_async_remote_copy(
            src_ref=ref, dst_ref=ref,
            send_sem=sib_send.at[p, slot], recv_sem=sib_recv.at[p, slot],
            device_id=sibling, device_id_type=MESH,
        )

    sent = []

    def go(copy):
        copy.start()
        sent.append(copy)

    lane = lax.broadcasted_iota(jnp.int32, (1, BLK), 1)

    def transpose_block(k):
        cols = pl.ds(pl.multiple_of(k * BLK, BLK), BLK)
        block = raw[:, :, cols].astype(F32)
        block = jnp.where((lane < counts[k])[None], block, 0.0)
        block = block.reshape(1024, BLK)
        trans[0] = block[:, :128]
        trans[1] = block[:, 128:]

        def one(c, carry):
            rows = pl.ds(c, 32, stride=32)
            pair = [trans[0, rows, :], trans[1, rows, :]]
            amp[k, c] = jnp.concatenate(pair, axis=1).astype(BF16)
            return carry

        lax.fori_loop(0, 32, one, 0, unroll=4)

    def transpose_blocks(first, last):
        def one(k, carry):
            transpose_block(k)
            return carry

        lax.fori_loop(first, last, one, 0)

    load_slab.wait()
    slab_copy = pltpu.make_async_remote_copy(
        src_ref=slab.at[:, :, half], dst_ref=slab.at[:, :, half],
        send_sem=fin_sem.at[0], recv_sem=fin_sem.at[1],
        device_id=sibling, device_id_type=MESH,
    )

    for phase in range(3):
        for p in range(3):
            dim = ORDERS[p][phase]
            k = pos[dim]
            right, left = neighbour(dim, 1), neighbour(dim, 3)
            if phase == 0:
                load_cyc[p].wait()
                go(piece(p, phase, k, None, 0, right))
                go(piece(p, phase, k, None, 1, left))
            else:
                go(piece(p, phase, k, 0, 0, right))
                go(piece(p, phase, k, 1, 1, left))
                go(piece(p, phase, k, 1, 2, right))
                go(piece(p, phase, k, 0, 3, left))
        if phase == 0:
            slab_copy.start()
            load_amp.wait()
            transpose_blocks(0, 1)
        if phase == 1:
            transpose_blocks(1, 3)
        if phase == 2:
            for p in range(3):
                dim = ORDERS[p][2]
                go(to_sibling(p, region(p, 2, pos[dim], None), 0))
            transpose_blocks(3, 8)
        for p in range(3):
            dim = ORDERS[p][phase]
            k = pos[dim]
            right, left = neighbour(dim, 1), neighbour(dim, 3)
            before, after = (k + 3) % 4, (k + 1) % 4
            if phase == 0:
                piece(p, phase, before, None, 0, right).wait_recv()
                piece(p, phase, after, None, 1, left).wait_recv()
                if p == 1:
                    go(piece(p, phase, after, None, 4, left))
                else:
                    go(piece(p, phase, before, None, 4, right))
            else:
                piece(p, phase, before, 0, 0, right).wait_recv()
                go(piece(p, phase, before, 0, 4, right))
                piece(p, phase, after, 1, 1, left).wait_recv()
                go(piece(p, phase, after, 1, 5, left))
        for p in range(3):
            dim = ORDERS[p][phase]
            k = pos[dim]
            right, left = neighbour(dim, 1), neighbour(dim, 3)
            before, after, far = (k + 3) % 4, (k + 1) % 4, (k + 2) % 4
            if phase > 0:
                piece(p, phase, before, 1, 2, right).wait_recv()
                piece(p, phase, after, 0, 3, left).wait_recv()
            if phase == 2:
                go(to_sibling(p, region(p, 2, before, None), 1))
                go(to_sibling(p, region(p, 2, after, None), 2))
        for p in range(3):
            dim = ORDERS[p][phase]
            k = pos[dim]
            right, left = neighbour(dim, 1), neighbour(dim, 3)
            far = (k + 2) % 4
            if phase == 0:
                piece(p, phase, far, None, 4, right).wait_recv()
            else:
                piece(p, phase, far, 0, 4, right).wait_recv()
                piece(p, phase, far, 1, 5, left).wait_recv()
            if phase == 2:
                go(to_sibling(p, region(p, 2, far, None), 3))
    for p in range(3):
        dim = ORDERS[p][2]
        k = pos[dim]
        for slot, at in enumerate((k, (k + 3) % 4, (k + 1) % 4, (k + 2) % 4)):
            done = ORDERS[p][:2]
            zhi, zlo = (ALL, ALL) if "z" in done else (at // 2, at % 2)
            xs = ALL if "x" in done else at
            ys = ALL if "y" in done else at
            ref = gs[p].at[zhi, xs, zlo, ys, 1 - core]
            to_sibling(p, ref, slot).wait_recv()
    for copy in sent:
        copy.wait_send()

    per = 32 // NR

    def a2a(r, j_to, src_h, h):
        cs = pl.ds(r * per, per)
        return pltpu.make_async_remote_copy(
            src_ref=dressed.at[h, cs], dst_ref=recv.at[src_h, cs],
            send_sem=a2a_send.at[r, h], recv_sem=a2a_recv.at[r, src_h],
            device_id=(occ, h * 2 + core), device_id_type=MESH,
        )

    def a2a_own(r):
        cs = pl.ds(r * per, per)
        return pltpu.make_async_copy(
            dressed.at[my_h, cs], recv.at[my_h, cs], a2a_recv.at[r, my_h]
        )

    def peer(j):
        return (zl + j // 4) % 2 * 4 + (y + j) % 4

    def dress(step, carry):
        r, j = step // 8, 7 - step % 8
        h = peer(j)
        block, high, low, bound = (table[i, h] for i in range(4))
        weights = jnp.concatenate(
            [g[high, low].reshape(BLK, w) for g, w in zip(gs, WIDTHS)], axis=1
        )
        cs = pl.ds(r * per, per)
        rows = jnp.concatenate([amp[i, cs].reshape(per * 32, BLK) for i in range(8)], axis=1)
        value = lax.dot_general(
            rows, weights, (((1,), (1,)), ((), ())), preferred_element_type=F32
        )
        value += amp[block, cs].reshape(per * 32, BLK).astype(F32)
        value = jnp.where(lane < bound, value, 0.0).astype(BF16)
        dressed[h, cs] = value.reshape(per, 32, BLK)

        @pl.when(j != 0)
        def _():
            a2a(r, j, my_h, h).start()

        @pl.when(j == 0)
        def _():
            a2a_own(r).start()

        return carry

    lax.fori_loop(0, NR * 8, dress, 0)

    slab_copy.wait_send()
    other = pl.ds(pl.multiple_of((1 - core) * 128, 128), 128)
    pltpu.make_async_remote_copy(
        src_ref=slab.at[:, :, other], dst_ref=slab.at[:, :, other],
        send_sem=fin_sem.at[0], recv_sem=fin_sem.at[1],
        device_id=sibling, device_id_type=MESH,
    ).wait_recv()
    total[...] = jnp.zeros_like(total)

    def ladder(r, carry):
        def arrived(j, inner):
            h = peer(j)
            a2a(r, j, h, h).wait_recv()
            return inner

        lax.fori_loop(1, 8, arrived, 0)
        a2a_own(r).wait()

        def one(c, inner):
            rows = recv[:, c].reshape(8 * 32, BLK)
            total[...] += jnp.dot(rows, slab[c], preferred_element_type=F32)
            return inner

        lax.fori_loop(r * per, (r + 1) * per, one, 0)
        return carry

    lax.fori_loop(0, NR, ladder, 0)

    live = lane < counts[my_h]
    result = jnp.where(live, total[...], 0.0).astype(BF16).reshape(8, 32, BLK)
    keep = jnp.where(core == 0, result[:, :, :128], result[:, :, 128:])
    give = jnp.where(core == 0, result[:, :, 128:], result[:, :, :128])
    mine[...] = give
    swap = pltpu.make_async_remote_copy(
        src_ref=mine, dst_ref=theirs, send_sem=fin_sem.at[2], recv_sem=fin_sem.at[3],
        device_id=sibling, device_id_type=MESH,
    )
    swap.start()
    out_ref[:, core] = keep

    def drain(step, carry):
        r, j = step // 7, 1 + step % 7
        a2a(r, j, my_h, peer(j)).wait_send()
        return carry

    lax.fori_loop(0, NR * 7, drain, 0)
    swap.wait()
    out_ref[:, 1 - core] = theirs[...]


def body(amplitudes, cycle_inter, ladder_slab, irrep_counts, slab_irrep):
    any_spec = pl.BlockSpec(memory_space=pl.ANY)
    smem = pl.BlockSpec(memory_space=pltpu.SMEM)
    dma = pltpu.SemaphoreType.DMA
    block = jnp.arange(8, dtype=jnp.int32) ^ slab_irrep[0]
    table = jnp.stack([block, block // 4, block % 4, irrep_counts[block]])
    out = pl.pallas_call(
        kernel,
        out_shape=jax.ShapeDtypeStruct((8, 2, 32, 128), BF16),
        in_specs=[any_spec, any_spec, any_spec, smem, smem],
        out_specs=pl.BlockSpec(memory_space=pltpu.VMEM),
        scratch_shapes=[
            pltpu.VMEM((32, 32, 2048), BF16),
            pltpu.VMEM((2, 1024, 128), F32),
            pltpu.VMEM((8, 32, 32, BLK), BF16),
        ]
        + [pltpu.VMEM((2, 4, 2, 4, 2, 16, w), BF16) for w in WIDTHS]
        + [
            pltpu.VMEM((8, 32, 32, BLK), BF16),
            pltpu.VMEM((8, 32, 32, BLK), BF16),
            pltpu.VMEM((32, BLK, BLK), BF16),
            pltpu.VMEM((BLK, BLK), F32),
            pltpu.VMEM((8, 32, 128), BF16),
            pltpu.VMEM((8, 32, 128), BF16),
            dma((5,)),
            dma((3, 3, 6)),
            dma((3, 3, 6)),
            dma((3, 4)),
            dma((3, 4)),
            dma((NR, 8)),
            dma((NR, 8)),
            dma((4,)),
        ],
        compiler_params=pltpu.CompilerParams(
            collective_id=0, has_side_effects=True, vmem_limit_bytes=56 * 1024 * 1024
        ),
        cost_estimate=pl.CostEstimate(
            flops=11 * 10**9, bytes_accessed=7 * 10**6, transcendentals=0
        ),
    )(amplitudes, cycle_inter.T, ladder_slab, irrep_counts, table)
    return out.reshape(512, 128)


def solution(mesh):
    placed = (
        P(("occ", "vir"), None, None),
        P(None, ("occ", "vir")),
        P(None, None, "vir"),
        P(),
        P(),
    )
    return jax.shard_map(
        body, mesh=mesh, in_specs=placed, out_specs=P("occ", "vir"), check_vma=False
    )
```

time: 673 us -> 104 us (0.15)
  the two profiles are of different devices: /device:TPU:1 before, /device:TPU:73 now
where the time goes in v1:
time: 104 us
  Pallas kernels  99.8 us (96%)
  local copies, waits for them, and re-layouts  2.87 us (3%)
    pallas_call x1, Pallas kernels, body(): pl.pallas_call(kernel, out_shape=jax.ShapeDtypeStruct((8, 2, 32, 128), BF...  99.8 us

profile of v1, /device:TPU:73, one launch (start us, length us, event | category | flops | bytes accessed | tf_op | source)
XLA Modules:
  0.0 104.0 jit_solution(15877301337135359660)
XLA Ops:
  0.7 1.3 %gather_fusion = s32[8]{0:T(128)S(1)} fusion(s32[8]{0:T(128)} %counts.1, s32[1024]{0:T(1024)S(1)} %pad_clamp_fusion), kind=kCustom, calls=%fused_computation | custom fusion | bytes 96 | tf_op jit(solution)/shard_map/gather | solution.py:327
  2.0 0.6 pad_add_fusion.table
  2.6 99.8 %shard_map.55 = bf16[8,2,32,128]{3,2,1,0:T(8,128)(2,1)} custom-call(bf16[32,32,2048]{2,1,0:T(8,128)(2,1)} %amp_hbm.1, bf16[16,2048]{1,0:T(8,128)(2,1)} %bitcast.11, bf16[32,256,128]{2,1,0:T(8,128)(2,1)} %slab_hbm.1, s32[8]{0:T(128)} %counts.1, s32[4,8]{1,0:T(4,128)} %pad_add_fusion.table), custom_call_target="tpu_custom_call" | custom-call | flops 11000000512 | bytes 7000000 | tf_op jit(solution)/shard_map/pallas_call | solution.py:328
  102.4 1.6 %copy.8 = bf16[512,128]{1,0:T(8,128)(2,1)} copy(bf16[512,128]{1,0:T(8,128)(2,1)} %bitcast.9) | data formatting | bytes 262144
  (4 shorter events, 0.0 us)

commit v2 on v1

--- a/solution.py
+++ b/solution.py
@@ -21,17 +21,20 @@
 
 def kernel(
     amp_hbm, cyc_hbm, slab_hbm, counts, table, out_ref,
-    raw, trans, amp, g0, g1, g2, dressed, recv, slab, total, mine, theirs,
-    local_sem, gather_send, gather_recv, sib_send, sib_recv, a2a_send, a2a_recv, fin_sem,
+    raw, trans, amp, g0, g1, g2, dressed, recv, slab, total, result, near, beyond,
+    local_sem, gather_send, gather_recv, sib_send, sib_recv, a2a_send, a2a_recv,
+    slab_send, slab_recv, fin_send, fin_recv,
 ):
     occ, vir = lax.axis_index("occ"), lax.axis_index("vir")
     x, y, core = occ % 4, vir // 2 % 4, vir % 2
     zh, zl = occ // 4, vir // 8
     z = zh * 2 + zl
-    my_h = vir // 2
     gs = (g0, g1, g2)
     pos = {"x": x, "y": y, "z": z}
     sibling = device(x, y, z, 1 - core)
+    z_inner = (z + 1 + 2 * zl) % 4
+    z_outer = (z + 3 + 2 * zl) % 4
+    z_of = (z, z_inner, z_outer)
 
     def neighbour(dim, step):
         at = dict(pos)
@@ -41,7 +44,7 @@
     load_amp = pltpu.make_async_copy(amp_hbm, raw, local_sem.at[0])
     load_amp.start()
     half = pl.ds(pl.multiple_of(core * 128, 128), 128)
-    load_slab = pltpu.make_async_copy(slab_hbm, slab.at[:, :, half], local_sem.at[1])
+    load_slab = pltpu.make_async_copy(slab_hbm, slab.at[0, :, :, half], local_sem.at[1])
     load_slab.start()
     offset = 0
     load_cyc = []
@@ -56,11 +59,13 @@
         offset += w
 
     barrier = pltpu.get_barrier_semaphore()
-    peers = [((my_h // 4 + j // 4) % 2) * 4 + (my_h + j) % 4 for j in range(8)]
     greet = [sibling, neighbour("x", 1), neighbour("x", 3)]
-    outer_z = (z + 3 + 2 * zl) % 4
-    greet.append(device(x, y, outer_z, core))
-    greet += [(occ, peers[j] * 2 + core) for j in range(1, 8)]
+    greet += [device(x, y, z_inner, core), device(x, y, z_outer, core)]
+    for step in (1, 3):
+        greet += [device(x, (y + step) % 4, zt, core) for zt in z_of]
+        greet.append(device(x, (y + step) % 4, z, 1 - core))
+    for step in (0, 1, 3):
+        greet += [device(x, (y + step) % 4, (z + 2) % 4, c) for c in range(2)]
     for who in greet:
         pl.semaphore_signal(barrier, inc=1, device_id=who, device_id_type=MESH)
     pl.semaphore_wait(barrier, len(greet))
@@ -137,12 +142,18 @@
 
         lax.fori_loop(first, last, one, 0)
 
+    def slab_piece(which, first, count, side, slot, who):
+        lanes = pl.ds(pl.multiple_of(side * 128, 128), 128)
+        src = slab.at[which[0], pl.ds(first, count), :, lanes]
+        dst = slab.at[which[1], pl.ds(first, count), :, lanes]
+        return pltpu.make_async_remote_copy(
+            src_ref=src, dst_ref=dst, send_sem=slab_send.at[slot], recv_sem=slab_recv.at[slot],
+            device_id=who, device_id_type=MESH,
+        )
+
     load_slab.wait()
-    slab_copy = pltpu.make_async_remote_copy(
-        src_ref=slab.at[:, :, half], dst_ref=slab.at[:, :, half],
-        send_sem=fin_sem.at[0], recv_sem=fin_sem.at[1],
-        device_id=sibling, device_id_type=MESH,
-    )
+    quarter = [(x + i) % 4 * 8 for i in range(4)]
+    x_right, x_left = neighbour("x", 1), neighbour("x", 3)
 
     for phase in range(3):
         for p in range(3):
@@ -159,7 +170,8 @@
                 go(piece(p, phase, k, 1, 2, right))
                 go(piece(p, phase, k, 0, 3, left))
         if phase == 0:
-            slab_copy.start()
+            go(slab_piece((0, 1), quarter[0], 8, core, 0, neighbour("y", 3)))
+            go(slab_piece((0, 0), 0, 32, core, 1, sibling))
             load_amp.wait()
             transpose_blocks(0, 1)
         if phase == 1:
@@ -219,104 +231,177 @@
             ys = ALL if "y" in done else at
             ref = gs[p].at[zhi, xs, zlo, ys, 1 - core]
             to_sibling(p, ref, slot).wait_recv()
+
+    slab_piece((0, 1), quarter[0], 8, core, 0, x_left).wait_recv()
+    go(slab_piece((1, 1), quarter[0], 8, core, 2, x_right))
+    go(slab_piece((1, 1), quarter[0], 8, core, 3, x_left))
+    go(slab_piece((1, 1), quarter[0], 8, core, 6, sibling))
+
+    per = 32 // NR
+    spots = ((0, 0), (1, 0), (1, 1), (0, 1))
+    y_of = (y, y, (y + 1) % 4, (y + 3) % 4)
+
+    def message(r, dy, zt):
+        cs = pl.ds(r * per, per)
+        src = dressed.at[int(zt > 0), dy, cs]
+        dst = recv.at[spots[dy][0], spots[dy][1], cs]
+        if zt == 0:
+            dst = recv.at[spots[dy][0], spots[dy][1], cs, pl.ds(0, 32)]
+        else:
+            src = dressed.at[1, dy, cs, pl.ds(16 * zt - 16, 16)]
+            dst = recv.at[spots[dy][0], spots[dy][1], cs, pl.ds(16 + 16 * zt, 16)]
+        return pltpu.make_async_remote_copy(
+            src_ref=src, dst_ref=dst,
+            send_sem=a2a_send.at[r, dy, zt], recv_sem=a2a_recv.at[r, dy, zt],
+            device_id=device(x, y_of[dy], z_of[zt], core), device_id_type=MESH,
+        )
+
+    def kinds(dys):
+        return [(dy, zt) for dy in dys for zt in range(3) if dy > 1 or zt > 0]
+
+    def dress(r, carry):
+        cs = pl.ds(r * per, per)
+        for dys in ((2, 3), (0, 1)):
+            blocks = [(dz, dy) for dy in dys for dz in range(2)]
+            tables = []
+            for dz, dy in blocks:
+                h = (zl + dz) % 2 * 4 + (y + dy) % 4
+                tables.append([table[i, h] for i in range(4)])
+            weights = jnp.concatenate(
+                [
+                    jnp.concatenate(
+                        [g[t[1], t[2]].reshape(BLK, w) for g, w in zip(gs, WIDTHS)], axis=1
+                    )
+                    for t in tables
+                ],
+                axis=0,
+            )
+            rows = jnp.concatenate([amp[i, cs].reshape(per * 32, BLK) for i in range(8)], axis=1)
+            values = lax.dot_general(
+                rows, weights, (((1,), (1,)), ((), ())), preferred_element_type=F32
+            )
+            for i, (dz, dy) in enumerate(blocks):
+                value = values[:, i * BLK : (i + 1) * BLK]
+                value += amp[tables[i][0], cs].reshape(per * 32, BLK).astype(F32)
+                value = jnp.where(lane < tables[i][3], value, 0.0).astype(BF16)
+                value = value.reshape(per, 32, BLK)
+                if dz == 0 and dy < 2:
+                    recv[spots[dy][0], spots[dy][1], cs, 0:32] = value
+                else:
+                    dressed[dz, dy, cs] = value
+            for dy, zt in kinds(dys):
+                message(r, dy, zt).start()
+
+        @pl.when(r == 2)
+        def _():
+            slab_piece((1, 1), quarter[3], 8, core, 2, x_right).wait_recv()
+            slab_piece((1, 1), quarter[3], 4, core, 4, x_right).start()
+            slab_piece((1, 1), quarter[1], 8, core, 3, x_left).wait_recv()
+            slab_piece((1, 1), quarter[1] + 4, 4, core, 5, x_left).start()
+            slab_piece((1, 1), quarter[3], 8, core, 7, sibling).start()
+            slab_piece((1, 1), quarter[1], 8, core, 8, sibling).start()
+
+        return carry
+
+    lax.fori_loop(0, NR, dress, 0)
+    sent.append(slab_piece((1, 1), quarter[3], 4, core, 4, x_right))
+    sent.append(slab_piece((1, 1), quarter[1] + 4, 4, core, 5, x_left))
+    sent.append(slab_piece((1, 1), quarter[3], 8, core, 7, sibling))
+    sent.append(slab_piece((1, 1), quarter[1], 8, core, 8, sibling))
+
+    slab_piece((0, 0), 0, 32, 1 - core, 1, sibling).wait_recv()
+    total[...] = jnp.zeros_like(total)
+
+    def ladder(r, half_of):
+        for dy in range(4):
+            if spots[dy][0] == half_of:
+                for kind in kinds((dy,)):
+                    message(r, *kind).wait_recv()
+        cs = pl.ds(r * per, per)
+        rows = jnp.concatenate(
+            [recv[half_of, :, r * per + c].reshape(128, BLK) for c in range(per)], axis=1
+        )
+        weights = slab[half_of, cs].reshape(per * BLK, BLK)
+        total[half_of] += jnp.dot(rows, weights, preferred_element_type=F32)
+
+    def ladder_first(r, carry):
+        ladder(r, 0)
+        return carry
+
+    def ladder_second(r, carry):
+        ladder(r, 1)
+        return carry
+
+    lax.fori_loop(0, NR - 1, ladder_first, 0)
+    slab_piece((1, 1), quarter[2], 4, core, 4, x_right).wait_recv()
+    slab_piece((1, 1), quarter[2] + 4, 4, core, 5, x_left).wait_recv()
+    go(slab_piece((1, 1), quarter[2], 8, core, 9, sibling))
+    for slot, q in ((6, 0), (7, 3), (8, 1), (9, 2)):
+        slab_piece((1, 1), quarter[q], 8, 1 - core, slot, sibling).wait_recv()
+    lax.fori_loop(0, NR - 1, ladder_second, 0)
+    ladder(NR - 1, 0)
+    ladder(NR - 1, 1)
+
+    def home(which, place, side):
+        at = device(x, (y + which) % 4, (z + 2 * place) % 4, side)
+        land = (near, beyond)[place].at[which, core]
+        rows = (pl.ds(0, 48), pl.ds(48, 16))[place]
+        return pltpu.make_async_remote_copy(
+            src_ref=result.at[which, side, :, rows], dst_ref=land,
+            send_sem=fin_send.at[which, place, side], recv_sem=fin_recv.at[which, place, core],
+            device_id=at, device_id_type=MESH,
+        )
+
+    for which in (1, 0):
+        h = zl * 4 + (y + which) % 4
+        value = jnp.where(lane < counts[h], total[which], 0.0).astype(BF16).reshape(2, 64, BLK)
+        for side in range(2):
+            result[which, side] = value[:, :, side * 128 : (side + 1) * 128]
+        for place in (1, 0):
+            for side in range(2):
+                if which == 0 and place == 0:
+                    @pl.when(core != side)
+                    def _():
+                        home(0, 0, side).start()
+                else:
+                    home(which, place, side).start()
+    near[0, core] = result[0, core, :, 0:48]
+
     for copy in sent:
         copy.wait_send()
 
-    per = 32 // NR
-
-    def a2a(r, j_to, src_h, h):
-        cs = pl.ds(r * per, per)
-        return pltpu.make_async_remote_copy(
-            src_ref=dressed.at[h, cs], dst_ref=recv.at[src_h, cs],
-            send_sem=a2a_send.at[r, h], recv_sem=a2a_recv.at[r, src_h],
-            device_id=(occ, h * 2 + core), device_id_type=MESH,
-        )
-
-    def a2a_own(r):
-        cs = pl.ds(r * per, per)
-        return pltpu.make_async_copy(
-            dressed.at[my_h, cs], recv.at[my_h, cs], a2a_recv.at[r, my_h]
-        )
-
-    def peer(j):
-        return (zl + j // 4) % 2 * 4 + (y + j) % 4
-
-    def dress(step, carry):
-        r, j = step // 8, 7 - step % 8
-        h = peer(j)
-        block, high, low, bound = (table[i, h] for i in range(4))
-        weights = jnp.concatenate(
-            [g[high, low].reshape(BLK, w) for g, w in zip(gs, WIDTHS)], axis=1
-        )
-        cs = pl.ds(r * per, per)
-        rows = jnp.concatenate([amp[i, cs].reshape(per * 32, BLK) for i in range(8)], axis=1)
-        value = lax.dot_general(
-            rows, weights, (((1,), (1,)), ((), ())), preferred_element_type=F32
-        )
-        value += amp[block, cs].reshape(per * 32, BLK).astype(F32)
-        value = jnp.where(lane < bound, value, 0.0).astype(BF16)
-        dressed[h, cs] = value.reshape(per, 32, BLK)
-
-        @pl.when(j != 0)
-        def _():
-            a2a(r, j, my_h, h).start()
-
-        @pl.when(j == 0)
-        def _():
-            a2a_own(r).start()
-
+    def drain(r, carry):
+        for dy, zt in kinds(range(4)):
+            message(r, dy, zt).wait_send()
         return carry
 
-    lax.fori_loop(0, NR * 8, dress, 0)
-
-    slab_copy.wait_send()
-    other = pl.ds(pl.multiple_of((1 - core) * 128, 128), 128)
-    pltpu.make_async_remote_copy(
-        src_ref=slab.at[:, :, other], dst_ref=slab.at[:, :, other],
-        send_sem=fin_sem.at[0], recv_sem=fin_sem.at[1],
-        device_id=sibling, device_id_type=MESH,
-    ).wait_recv()
-    total[...] = jnp.zeros_like(total)
-
-    def ladder(r, carry):
-        def arrived(j, inner):
-            h = peer(j)
-            a2a(r, j, h, h).wait_recv()
-            return inner
-
-        lax.fori_loop(1, 8, arrived, 0)
-        a2a_own(r).wait()
-
-        def one(c, inner):
-            rows = recv[:, c].reshape(8 * 32, BLK)
-            total[...] += jnp.dot(rows, slab[c], preferred_element_type=F32)
-            return inner
-
-        lax.fori_loop(r * per, (r + 1) * per, one, 0)
-        return carry
-
-    lax.fori_loop(0, NR, ladder, 0)
-
-    live = lane < counts[my_h]
-    result = jnp.where(live, total[...], 0.0).astype(BF16).reshape(8, 32, BLK)
-    keep = jnp.where(core == 0, result[:, :, :128], result[:, :, 128:])
-    give = jnp.where(core == 0, result[:, :, 128:], result[:, :, :128])
-    mine[...] = give
-    swap = pltpu.make_async_remote_copy(
-        src_ref=mine, dst_ref=theirs, send_sem=fin_sem.at[2], recv_sem=fin_sem.at[3],
-        device_id=sibling, device_id_type=MESH,
-    )
-    swap.start()
-    out_ref[:, core] = keep
-
-    def drain(step, carry):
-        r, j = step // 7, 1 + step % 7
-        a2a(r, j, my_h, peer(j)).wait_send()
-        return carry
-
-    lax.fori_loop(0, NR * 7, drain, 0)
-    swap.wait()
-    out_ref[:, 1 - core] = theirs[...]
+    lax.fori_loop(0, NR, drain, 0)
+
+    def arrival(which, place, side):
+        land = (near, beyond)[place].at[which, side]
+        rows = (pl.ds(0, 48), pl.ds(48, 16))[place]
+        return pltpu.make_async_remote_copy(
+            src_ref=result.at[which, side, :, rows], dst_ref=land,
+            send_sem=fin_send.at[which, place, side], recv_sem=fin_recv.at[which, place, side],
+            device_id=sibling, device_id_type=MESH,
+        )
+
+    for which in range(2):
+        for place in range(2):
+            for side in range(2):
+                if which == 0 and place == 0:
+                    @pl.when(core != side)
+                    def _():
+                        arrival(0, 0, side).wait()
+                else:
+                    arrival(which, place, side).wait()
+    for which in range(2):
+        for other in range(2):
+            source = (y + ((0, 1), (3, 2))[which][other]) % 4
+            for side in range(2):
+                out_ref[zl, source, side] = near[which, side, other, 0:32]
+                out_ref[1 - zl, source, side, 0:16] = near[which, side, other, 32:48]
+                out_ref[1 - zl, source, side, 16:32] = beyond[which, side, other]
 
 
 def body(amplitudes, cycle_inter, ladder_slab, irrep_counts, slab_irrep):
@@ -327,7 +412,7 @@
     table = jnp.stack([block, block // 4, block % 4, irrep_counts[block]])
     out = pl.pallas_call(
         kernel,
-        out_shape=jax.ShapeDtypeStruct((8, 2, 32, 128), BF16),
+        out_shape=jax.ShapeDtypeStruct((2, 4, 2, 32, 128), BF16),
         in_specs=[any_spec, any_spec, any_spec, smem, smem],
         out_specs=pl.BlockSpec(memory_space=pltpu.VMEM),
         scratch_shapes=[
@@ -337,20 +422,24 @@
         ]
         + [pltpu.VMEM((2, 4, 2, 4, 2, 16, w), BF16) for w in WIDTHS]
         + [
-            pltpu.VMEM((8, 32, 32, BLK), BF16),
-            pltpu.VMEM((8, 32, 32, BLK), BF16),
-            pltpu.VMEM((32, BLK, BLK), BF16),
-            pltpu.VMEM((BLK, BLK), F32),
-            pltpu.VMEM((8, 32, 128), BF16),
-            pltpu.VMEM((8, 32, 128), BF16),
+            pltpu.VMEM((2, 4, 32, 32, BLK), BF16),
+            pltpu.VMEM((2, 2, 32, 64, BLK), BF16),
+            pltpu.VMEM((2, 32, BLK, BLK), BF16),
+            pltpu.VMEM((2, 128, BLK), F32),
+            pltpu.VMEM((2, 2, 2, 64, 128), BF16),
+            pltpu.VMEM((2, 2, 2, 48, 128), BF16),
+            pltpu.VMEM((2, 2, 2, 16, 128), BF16),
             dma((5,)),
             dma((3, 3, 6)),
             dma((3, 3, 6)),
             dma((3, 4)),
             dma((3, 4)),
-            dma((NR, 8)),
-            dma((NR, 8)),
-            dma((4,)),
+            dma((NR, 4, 3)),
+            dma((NR, 4, 3)),
+            dma((10,)),
+            dma((10,)),
+            dma((2, 2, 2)),
+            dma((2, 2, 2)),
         ],
         compiler_params=pltpu.CompilerParams(
             collective_id=0, has_side_effects=True, vmem_limit_bytes=56 * 1024 * 1024

time: 104 us -> 81.1 us (0.78)
  the two profiles are of different devices: /device:TPU:73 before, /device:TPU:1 now
where the time goes in v2:
time: 81.1 us; the launch traced here: 81 us
  Pallas kernels  76.8 us (95%)
  local copies, waits for them, and re-layouts  2.87 us (4%)
    pallas_call x1, Pallas kernels, body(): pl.pallas_call(kernel, out_shape=jax.ShapeDtypeStruct((2, 4, 2, 32, 128),...  76.8 us

profile of v2, /device:TPU:1, one launch (start us, length us, event | category | flops | bytes accessed | tf_op | source)
XLA Modules:
  0.0 81.0 jit_solution(9960995171074099758)
XLA Ops:
  0.7 1.3 %gather_fusion = s32[8]{0:T(128)S(1)} fusion(s32[8]{0:T(128)} %counts.1, s32[1024]{0:T(1024)S(1)} %pad_clamp_fusion), kind=kCustom, calls=%fused_computation | custom fusion | bytes 96 | tf_op jit(solution)/shard_map/gather | solution.py:412
  2.0 0.6 pad_add_fusion.table
  2.6 76.8 %shard_map.55 = bf16[2,4,2,32,128]{4,3,2,1,0:T(8,128)(2,1)} custom-call(bf16[32,32,2048]{2,1,0:T(8,128)(2,1)} %amp_hbm.1, bf16[16,2048]{1,0:T(8,128)(2,1)} %bitcast.11, bf16[32,256,128]{2,1,0:T(8,128)(2,1)} %slab_hbm.1, s32[8]{0:T(128)} %counts.1, s32[4,8]{1,0:T(4,128)} %pad_add_fusion.table), custom_call_target="tpu_custom_call" | custom-call | flops 11000000512 | bytes 7000000 | tf_op jit(solution)/shard_map/pallas_call | solution.py:413
  79.4 1.6 %copy.8 = bf16[512,128]{1,0:T(8,128)(2,1)} copy(bf16[512,128]{1,0:T(8,128)(2,1)} %bitcast.9) | data formatting | bytes 262144
  (4 shorter events, 0.0 us)

commit v3 on v2

--- a/solution.py
+++ b/solution.py
@@ -6,7 +6,7 @@
 from jax.sharding import PartitionSpec as P
 
 BLK = 256
-WIDTHS = (768, 640, 640)
+WIDTHS = (896, 256, 896)
 ORDERS = ("yzx", "zxy", "xyz")
 NR = 4
 MESH = pl.DeviceIdType.MESH
@@ -59,52 +59,31 @@
         offset += w
 
     barrier = pltpu.get_barrier_semaphore()
-    greet = [sibling, neighbour("x", 1), neighbour("x", 3)]
-    greet += [device(x, y, z_inner, core), device(x, y, z_outer, core)]
-    for step in (1, 3):
-        greet += [device(x, (y + step) % 4, zt, core) for zt in z_of]
-        greet.append(device(x, (y + step) % 4, z, 1 - core))
-    for step in (0, 1, 3):
-        greet += [device(x, (y + step) % 4, (z + 2) % 4, c) for c in range(2)]
+    greet = [sibling] + [neighbour(dim, step) for dim in "xyz" for step in (1, 3, 2)]
     for who in greet:
         pl.semaphore_signal(barrier, inc=1, device_id=who, device_id_type=MESH)
     pl.semaphore_wait(barrier, len(greet))
 
-    def region(p, phase, k, part):
-        done = ORDERS[p][:phase]
-        dim = ORDERS[p][phase]
-        at = {}
-        for name in "xyz":
-            at[name] = ALL if name in done else pos[name]
-        at[dim] = k
-        zhi, zlo = (ALL, ALL) if "z" in done else (at["z"] // 2, at["z"] % 2)
-        xs, ys = at["x"], at["y"]
-        if part is not None and phase > 0:
-            if "z" in done:
-                zhi = part
-            elif "x" in done:
-                xs = pl.ds(2 * part, 2)
-            else:
-                ys = pl.ds(2 * part, 2)
-        return gs[p].at[zhi, xs, zlo, ys, core]
-
-    def piece(p, phase, k, part, slot, who):
-        ref = region(p, phase, k, part)
+    def region(p, second, third, part, side):
+        d1, d2, d3 = ORDERS[p]
+        at = {d1: ALL if part is None else pl.ds(2 * part, 2), d2: second, d3: third}
+        zhi, zlo = at["z"] // 2 if at["z"] is not ALL and d1 != "z" else ALL, ALL
+        if d1 == "z":
+            zhi = ALL if part is None else part
+        elif at["z"] is not ALL:
+            zlo = at["z"] % 2
+        return gs[p].at[zhi, at["x"], zlo, at["y"], side]
+
+    def pass_on(p, second, third, part, slot, who):
+        ref = region(p, second, third, part, core)
         return pltpu.make_async_remote_copy(
             src_ref=ref, dst_ref=ref,
-            send_sem=gather_send.at[p, phase, slot], recv_sem=gather_recv.at[p, phase, slot],
+            send_sem=gather_send.at[p, slot], recv_sem=gather_recv.at[p, slot],
             device_id=who, device_id_type=MESH,
         )
 
-    def to_sibling(p, ref, slot):
-        return pltpu.make_async_remote_copy(
-            src_ref=ref, dst_ref=ref,
-            send_sem=sib_send.at[p, slot], recv_sem=sib_recv.at[p, slot],
-            device_id=sibling, device_id_type=MESH,
-        )
-
-    def sib_wait(p, ref_of, slot):
-        ref = ref_of
+    def to_sibling(p, second, third, slot, side):
+        ref = region(p, second, third, None, side)
         return pltpu.make_async_remote_copy(
             src_ref=ref, dst_ref=ref,
             send_sem=sib_send.at[p, slot], recv_sem=sib_recv.at[p, slot],
@@ -151,87 +130,99 @@
             device_id=who, device_id_type=MESH,
         )
 
-    load_slab.wait()
     quarter = [(x + i) % 4 * 8 for i in range(4)]
     x_right, x_left = neighbour("x", 1), neighbour("x", 3)
 
-    for phase in range(3):
+    def first(p, step, source):
+        d1 = ORDERS[p][0]
+        at = dict(pos)
+        at[d1] = (at[d1] + source) % 4
+        ref = gs[p].at[at["z"] // 2, at["x"], at["z"] % 2, at["y"], core]
+        return pltpu.make_async_remote_copy(
+            src_ref=ref, dst_ref=ref,
+            send_sem=gather_send.at[p, step - 1], recv_sem=gather_recv.at[p, step - 1],
+            device_id=neighbour(d1, step), device_id_type=MESH,
+        )
+
+    offsets = (0, 3, 1, 2)
+    seconds = [[(pos[ORDERS[p][1]] + i) % 4 for i in offsets] for p in range(3)]
+    thirds = [[(pos[ORDERS[p][2]] + i) % 4 for i in offsets] for p in range(3)]
+    ends = [
+        [(neighbour(ORDERS[p][i], 1), neighbour(ORDERS[p][i], 3)) for i in range(3)]
+        for p in range(3)
+    ]
+
+    def along_second(p, i, part, slot):
+        return pass_on(p, seconds[p][i], thirds[p][0], part, 3 + slot, ends[p][1][slot % 2])
+
+    def along_third(p, sub, i, part, slot):
+        return pass_on(p, seconds[p][sub], thirds[p][i], part, 7 + 4 * sub + slot, ends[p][2][slot % 2])
+
+    def spread(p, sub):
+        go(along_third(p, sub, 0, None, 0))
+        go(along_third(p, sub, 0, None, 1))
+
+    def forward_third(p, sub):
+        along_third(p, sub, 1, None, 0).wait_recv()
+        go(along_third(p, sub, 1, 0, 2))
+        along_third(p, sub, 2, None, 1).wait_recv()
+        go(along_third(p, sub, 2, 1, 3))
+
+    def slab_fetch(first, slot):
+        lanes = pl.ds(pl.multiple_of(core * 128, 128), 128)
+        return pltpu.make_async_remote_copy(
+            src_ref=slab_hbm.at[pl.ds(first, 8)], dst_ref=slab.at[1, pl.ds(first, 8), :, lanes],
+            send_sem=slab_send.at[slot], recv_sem=slab_recv.at[slot],
+            device_id=neighbour("y", 3), device_id_type=MESH,
+        )
+
+    for p in range(3):
+        load_cyc[p].wait()
+        for step in (1, 3, 2):
+            go(first(p, step, 0))
+    load_amp.wait()
+    transpose_blocks(0, 1)
+    for p in range(3):
+        for step in (1, 3, 2):
+            first(p, step, 4 - step).wait_recv()
+        go(along_second(p, 0, None, 0))
+        go(along_second(p, 0, None, 1))
+        spread(p, 0)
+    load_slab.wait()
+    go(slab_piece((0, 0), 0, 32, core, 1, sibling))
+    transpose_blocks(1, 3)
+    for p in range(3):
+        along_second(p, 1, None, 0).wait_recv()
+        go(along_second(p, 1, 0, 2))
+        spread(p, 1)
+        along_second(p, 2, None, 1).wait_recv()
+        go(along_second(p, 2, 1, 3))
+        spread(p, 2)
+    for p in range(3):
+        forward_third(p, 0)
+    for p in range(3):
+        along_second(p, 3, 0, 2).wait_recv()
+        along_second(p, 3, 1, 3).wait_recv()
+        spread(p, 3)
+        go(to_sibling(p, ALL, thirds[p][0], 0, core))
+    go(slab_fetch(quarter[0], 0))
+    transpose_blocks(3, 8)
+    for sub in (1, 2, 3):
         for p in range(3):
-            dim = ORDERS[p][phase]
-            k = pos[dim]
-            right, left = neighbour(dim, 1), neighbour(dim, 3)
-            if phase == 0:
-                load_cyc[p].wait()
-                go(piece(p, phase, k, None, 0, right))
-                go(piece(p, phase, k, None, 1, left))
-            else:
-                go(piece(p, phase, k, 0, 0, right))
-                go(piece(p, phase, k, 1, 1, left))
-                go(piece(p, phase, k, 1, 2, right))
-                go(piece(p, phase, k, 0, 3, left))
-        if phase == 0:
-            go(slab_piece((0, 1), quarter[0], 8, core, 0, neighbour("y", 3)))
-            go(slab_piece((0, 0), 0, 32, core, 1, sibling))
-            load_amp.wait()
-            transpose_blocks(0, 1)
-        if phase == 1:
-            transpose_blocks(1, 3)
-        if phase == 2:
-            for p in range(3):
-                dim = ORDERS[p][2]
-                go(to_sibling(p, region(p, 2, pos[dim], None), 0))
-            transpose_blocks(3, 8)
+            forward_third(p, sub)
+    for p in range(3):
+        go(to_sibling(p, ALL, thirds[p][1], 1, core))
+        go(to_sibling(p, ALL, thirds[p][2], 2, core))
+    for sub in range(4):
         for p in range(3):
-            dim = ORDERS[p][phase]
-            k = pos[dim]
-            right, left = neighbour(dim, 1), neighbour(dim, 3)
-            before, after = (k + 3) % 4, (k + 1) % 4
-            if phase == 0:
-                piece(p, phase, before, None, 0, right).wait_recv()
-                piece(p, phase, after, None, 1, left).wait_recv()
-                if p == 1:
-                    go(piece(p, phase, after, None, 4, left))
-                else:
-                    go(piece(p, phase, before, None, 4, right))
-            else:
-                piece(p, phase, before, 0, 0, right).wait_recv()
-                go(piece(p, phase, before, 0, 4, right))
-                piece(p, phase, after, 1, 1, left).wait_recv()
-                go(piece(p, phase, after, 1, 5, left))
-        for p in range(3):
-            dim = ORDERS[p][phase]
-            k = pos[dim]
-            right, left = neighbour(dim, 1), neighbour(dim, 3)
-            before, after, far = (k + 3) % 4, (k + 1) % 4, (k + 2) % 4
-            if phase > 0:
-                piece(p, phase, before, 1, 2, right).wait_recv()
-                piece(p, phase, after, 0, 3, left).wait_recv()
-            if phase == 2:
-                go(to_sibling(p, region(p, 2, before, None), 1))
-                go(to_sibling(p, region(p, 2, after, None), 2))
-        for p in range(3):
-            dim = ORDERS[p][phase]
-            k = pos[dim]
-            right, left = neighbour(dim, 1), neighbour(dim, 3)
-            far = (k + 2) % 4
-            if phase == 0:
-                piece(p, phase, far, None, 4, right).wait_recv()
-            else:
-                piece(p, phase, far, 0, 4, right).wait_recv()
-                piece(p, phase, far, 1, 5, left).wait_recv()
-            if phase == 2:
-                go(to_sibling(p, region(p, 2, far, None), 3))
-    for p in range(3):
-        dim = ORDERS[p][2]
-        k = pos[dim]
-        for slot, at in enumerate((k, (k + 3) % 4, (k + 1) % 4, (k + 2) % 4)):
-            done = ORDERS[p][:2]
-            zhi, zlo = (ALL, ALL) if "z" in done else (at // 2, at % 2)
-            xs = ALL if "x" in done else at
-            ys = ALL if "y" in done else at
-            ref = gs[p].at[zhi, xs, zlo, ys, 1 - core]
-            to_sibling(p, ref, slot).wait_recv()
-
+            along_third(p, sub, 3, 0, 2).wait_recv()
+            along_third(p, sub, 3, 1, 3).wait_recv()
+            go(to_sibling(p, seconds[p][sub], thirds[p][3], 3 + sub, core))
+    for p in range(3):
+        for i in range(3):
+            to_sibling(p, ALL, thirds[p][i], i, 1 - core).wait_recv()
+        for sub in range(4):
+            to_sibling(p, seconds[p][sub], thirds[p][3], 3 + sub, 1 - core).wait_recv()
     slab_piece((0, 1), quarter[0], 8, core, 0, x_left).wait_recv()
     go(slab_piece((1, 1), quarter[0], 8, core, 2, x_right))
     go(slab_piece((1, 1), quarter[0], 8, core, 3, x_left))
@@ -266,7 +257,7 @@
             tables = []
             for dz, dy in blocks:
                 h = (zl + dz) % 2 * 4 + (y + dy) % 4
-                tables.append([table[i, h] for i in range(4)])
+                tables.append([table[i, h] for i in range(3)])
             weights = jnp.concatenate(
                 [
                     jnp.concatenate(
@@ -283,7 +274,7 @@
             for i, (dz, dy) in enumerate(blocks):
                 value = values[:, i * BLK : (i + 1) * BLK]
                 value += amp[tables[i][0], cs].reshape(per * 32, BLK).astype(F32)
-                value = jnp.where(lane < tables[i][3], value, 0.0).astype(BF16)
+                value = jnp.where(lane < counts[tables[i][0]], value, 0.0).astype(BF16)
                 value = value.reshape(per, 32, BLK)
                 if dz == 0 and dy < 2:
                     recv[spots[dy][0], spots[dy][1], cs, 0:32] = value
@@ -408,8 +399,9 @@
     any_spec = pl.BlockSpec(memory_space=pl.ANY)
     smem = pl.BlockSpec(memory_space=pltpu.SMEM)
     dma = pltpu.SemaphoreType.DMA
-    block = jnp.arange(8, dtype=jnp.int32) ^ slab_irrep[0]
-    table = jnp.stack([block, block // 4, block % 4, irrep_counts[block]])
+    block = lax.broadcasted_iota(jnp.int32, (3, 8), 1) ^ slab_irrep[0]
+    row = lax.broadcasted_iota(jnp.int32, (3, 8), 0)
+    table = jnp.where(row == 0, block, jnp.where(row == 1, block >> 2, block & 3))
     out = pl.pallas_call(
         kernel,
         out_shape=jax.ShapeDtypeStruct((2, 4, 2, 32, 128), BF16),
@@ -430,10 +422,10 @@
             pltpu.VMEM((2, 2, 2, 48, 128), BF16),
             pltpu.VMEM((2, 2, 2, 16, 128), BF16),
             dma((5,)),
-            dma((3, 3, 6)),
-            dma((3, 3, 6)),
-            dma((3, 4)),
-            dma((3, 4)),
+            dma((3, 23)),
+            dma((3, 23)),
+            dma((3, 7)),
+            dma((3, 7)),
             dma((NR, 4, 3)),
             dma((NR, 4, 3)),
             dma((10,)),

time: 81.1 us -> 75.7 us (0.933)
  Pallas kernels: 76.8 us -> 72.7 us
  local copies, waits for them, and re-layouts: 2.87 us -> 1.57 us
    pallas_call x1, Pallas kernels: 76.8 us -> 72.7 us  [body(): pl.pallas_call(kernel, out_shape=jax.ShapeDtypeStruct((2, 4, 2, 32, 128),...]
    gather x1 -> x0, local copies, waits for them, and re-layouts: 1.3 us -> none  [body(): table = jnp.stack([block, block // 4, block % 4, irrep_counts[block]])]
where the time goes in v3:
time: 75.7 us; the launch traced here: 75.6 us
  Pallas kernels  72.7 us (96%)
  local copies, waits for them, and re-layouts  1.57 us (2%)
    pallas_call x1, Pallas kernels, body(): pl.pallas_call(kernel, out_shape=jax.ShapeDtypeStruct((2, 4, 2, 32, 128),...  72.7 us
    unnamed x1, local copies, waits for them, and re-layouts  1.57 us

profile of v3, /device:TPU:1, one launch (start us, length us, event | category | flops | bytes accessed | tf_op | source)
XLA Modules:
  0.0 75.6 jit_solution(17378015541326503451)
XLA Ops:
  0.7 0.7 select_select_fusion.table
  1.3 72.7 %shard_map.55 = bf16[2,4,2,32,128]{4,3,2,1,0:T(8,128)(2,1)} custom-call(bf16[32,32,2048]{2,1,0:T(8,128)(2,1)} %amp_hbm.1, bf16[16,2048]{1,0:T(8,128)(2,1)} %bitcast.6, bf16[32,256,128]{2,1,0:T(8,128)(2,1)} %slab_hbm.1, s32[8]{0:T(128)} %counts.1, s32[3,8]{1,0:T(4,128)} %select_select_fusion.table), custom_call_target="tpu_custom_call" | custom-call | flops 11000000512 | bytes 7000000 | tf_op jit(solution)/shard_map/pallas_call | solution.py:405
  74.0 1.6 %copy.8 = bf16[512,128]{1,0:T(8,128)(2,1)} copy(bf16[512,128]{1,0:T(8,128)(2,1)} %bitcast.5) | data formatting | bytes 262144
  (3 shorter events, 0.0 us)

commit v4 on v3

--- a/solution.py
+++ b/solution.py
@@ -6,7 +6,7 @@
 from jax.sharding import PartitionSpec as P
 
 BLK = 256
-WIDTHS = (896, 256, 896)
+WIDTHS = (768, 512, 768)
 ORDERS = ("yzx", "zxy", "xyz")
 NR = 4
 MESH = pl.DeviceIdType.MESH
@@ -147,26 +147,19 @@
     offsets = (0, 3, 1, 2)
     seconds = [[(pos[ORDERS[p][1]] + i) % 4 for i in offsets] for p in range(3)]
     thirds = [[(pos[ORDERS[p][2]] + i) % 4 for i in offsets] for p in range(3)]
-    ends = [
-        [(neighbour(ORDERS[p][i], 1), neighbour(ORDERS[p][i], 3)) for i in range(3)]
-        for p in range(3)
-    ]
-
-    def along_second(p, i, part, slot):
-        return pass_on(p, seconds[p][i], thirds[p][0], part, 3 + slot, ends[p][1][slot % 2])
-
-    def along_third(p, sub, i, part, slot):
-        return pass_on(p, seconds[p][sub], thirds[p][i], part, 7 + 4 * sub + slot, ends[p][2][slot % 2])
+    steps = (1, 3, 2)
+
+    def along_second(p, i, slot):
+        who = neighbour(ORDERS[p][1], steps[slot])
+        return pass_on(p, seconds[p][i], thirds[p][0], None, 3 + slot, who)
+
+    def along_third(p, sub, i, slot):
+        who = neighbour(ORDERS[p][2], steps[slot])
+        return pass_on(p, seconds[p][sub], thirds[p][i], None, 6 + 3 * sub + slot, who)
 
     def spread(p, sub):
-        go(along_third(p, sub, 0, None, 0))
-        go(along_third(p, sub, 0, None, 1))
-
-    def forward_third(p, sub):
-        along_third(p, sub, 1, None, 0).wait_recv()
-        go(along_third(p, sub, 1, 0, 2))
-        along_third(p, sub, 2, None, 1).wait_recv()
-        go(along_third(p, sub, 2, 1, 3))
+        for slot in range(3):
+            go(along_third(p, sub, 0, slot))
 
     def slab_fetch(first, slot):
         lanes = pl.ds(pl.multiple_of(core * 128, 128), 128)
@@ -178,56 +171,33 @@
 
     for p in range(3):
         load_cyc[p].wait()
-        for step in (1, 3, 2):
+        for step in steps:
             go(first(p, step, 0))
     load_amp.wait()
     transpose_blocks(0, 1)
     for p in range(3):
-        for step in (1, 3, 2):
+        for step in steps:
             first(p, step, 4 - step).wait_recv()
-        go(along_second(p, 0, None, 0))
-        go(along_second(p, 0, None, 1))
+        for slot in range(3):
+            go(along_second(p, 0, slot))
         spread(p, 0)
     load_slab.wait()
     go(slab_piece((0, 0), 0, 32, core, 1, sibling))
     transpose_blocks(1, 3)
-    for p in range(3):
-        along_second(p, 1, None, 0).wait_recv()
-        go(along_second(p, 1, 0, 2))
-        spread(p, 1)
-        along_second(p, 2, None, 1).wait_recv()
-        go(along_second(p, 2, 1, 3))
-        spread(p, 2)
-    for p in range(3):
-        forward_third(p, 0)
-    for p in range(3):
-        along_second(p, 3, 0, 2).wait_recv()
-        along_second(p, 3, 1, 3).wait_recv()
-        spread(p, 3)
-        go(to_sibling(p, ALL, thirds[p][0], 0, core))
+    for slot in range(3):
+        for p in range(3):
+            along_second(p, slot + 1, slot).wait_recv()
+            spread(p, slot + 1)
     go(slab_fetch(quarter[0], 0))
     transpose_blocks(3, 8)
-    for sub in (1, 2, 3):
-        for p in range(3):
-            forward_third(p, sub)
-    for p in range(3):
-        go(to_sibling(p, ALL, thirds[p][1], 1, core))
-        go(to_sibling(p, ALL, thirds[p][2], 2, core))
     for sub in range(4):
         for p in range(3):
-            along_third(p, sub, 3, 0, 2).wait_recv()
-            along_third(p, sub, 3, 1, 3).wait_recv()
-            go(to_sibling(p, seconds[p][sub], thirds[p][3], 3 + sub, core))
+            for slot in range(3):
+                along_third(p, sub, slot + 1, slot).wait_recv()
+            go(to_sibling(p, seconds[p][sub], ALL, sub, core))
     for p in range(3):
-        for i in range(3):
-            to_sibling(p, ALL, thirds[p][i], i, 1 - core).wait_recv()
         for sub in range(4):
-            to_sibling(p, seconds[p][sub], thirds[p][3], 3 + sub, 1 - core).wait_recv()
-    slab_piece((0, 1), quarter[0], 8, core, 0, x_left).wait_recv()
-    go(slab_piece((1, 1), quarter[0], 8, core, 2, x_right))
-    go(slab_piece((1, 1), quarter[0], 8, core, 3, x_left))
-    go(slab_piece((1, 1), quarter[0], 8, core, 6, sibling))
-
+            to_sibling(p, seconds[p][sub], ALL, sub, 1 - core).wait_recv()
     per = 32 // NR
     spots = ((0, 0), (1, 0), (1, 1), (0, 1))
     y_of = (y, y, (y + 1) % 4, (y + 3) % 4)
@@ -283,7 +253,14 @@
             for dy, zt in kinds(dys):
                 message(r, dy, zt).start()
 
-        @pl.when(r == 2)
+        @pl.when(r == 0)
+        def _():
+            slab_piece((0, 1), quarter[0], 8, core, 0, x_left).wait_recv()
+            slab_piece((1, 1), quarter[0], 8, core, 2, x_right).start()
+            slab_piece((1, 1), quarter[0], 8, core, 3, x_left).start()
+            slab_piece((1, 1), quarter[0], 8, core, 6, sibling).start()
+
+        @pl.when(r == 3)
         def _():
             slab_piece((1, 1), quarter[3], 8, core, 2, x_right).wait_recv()
             slab_piece((1, 1), quarter[3], 4, core, 4, x_right).start()
@@ -295,6 +272,9 @@
         return carry
 
     lax.fori_loop(0, NR, dress, 0)
+    sent.append(slab_piece((1, 1), quarter[0], 8, core, 2, x_right))
+    sent.append(slab_piece((1, 1), quarter[0], 8, core, 3, x_left))
+    sent.append(slab_piece((1, 1), quarter[0], 8, core, 6, sibling))
     sent.append(slab_piece((1, 1), quarter[3], 4, core, 4, x_right))
     sent.append(slab_piece((1, 1), quarter[1] + 4, 4, core, 5, x_left))
     sent.append(slab_piece((1, 1), quarter[3], 8, core, 7, sibling))
@@ -330,9 +310,6 @@
     for slot, q in ((6, 0), (7, 3), (8, 1), (9, 2)):
         slab_piece((1, 1), quarter[q], 8, 1 - core, slot, sibling).wait_recv()
     lax.fori_loop(0, NR - 1, ladder_second, 0)
-    ladder(NR - 1, 0)
-    ladder(NR - 1, 1)
-
     def home(which, place, side):
         at = device(x, (y + which) % 4, (z + 2 * place) % 4, side)
         land = (near, beyond)[place].at[which, core]
@@ -344,6 +321,7 @@
         )
 
     for which in (1, 0):
+        ladder(NR - 1, which)
         h = zl * 4 + (y + which) % 4
         value = jnp.where(lane < counts[h], total[which], 0.0).astype(BF16).reshape(2, 64, BLK)
         for side in range(2):
@@ -422,10 +400,10 @@
             pltpu.VMEM((2, 2, 2, 48, 128), BF16),
             pltpu.VMEM((2, 2, 2, 16, 128), BF16),
             dma((5,)),
-            dma((3, 23)),
-            dma((3, 23)),
-            dma((3, 7)),
-            dma((3, 7)),
+            dma((3, 18)),
+            dma((3, 18)),
+            dma((3, 4)),
+            dma((3, 4)),
             dma((NR, 4, 3)),
             dma((NR, 4, 3)),
             dma((10,)),

time: 75.7 us -> 74.1 us (0.979)
  Pallas kernels: 72.7 us -> 71 us
    pallas_call x1, Pallas kernels: 72.7 us -> 71 us  [body(): pl.pallas_call(kernel, out_shape=jax.ShapeDtypeStruct((2, 4, 2, 32, 128),...]
where the time goes in v4:
time: 74.1 us; the launch traced here: 73.9 us
  Pallas kernels  71 us (96%)
  local copies, waits for them, and re-layouts  1.57 us (2%)
    pallas_call x1, Pallas kernels, body(): pl.pallas_call(kernel, out_shape=jax.ShapeDtypeStruct((2, 4, 2, 32, 128),...  71 us
    unnamed x1, local copies, waits for them, and re-layouts  1.57 us

profile of v4, /device:TPU:1, one launch (start us, length us, event | category | flops | bytes accessed | tf_op | source)
XLA Modules:
  0.0 73.9 jit_solution(2891448497066458755)
XLA Ops:
  0.7 0.7 select_select_fusion.table
  1.3 71.0 %shard_map.55 = bf16[2,4,2,32,128]{4,3,2,1,0:T(8,128)(2,1)} custom-call(bf16[32,32,2048]{2,1,0:T(8,128)(2,1)} %amp_hbm.1, bf16[16,2048]{1,0:T(8,128)(2,1)} %bitcast.6, bf16[32,256,128]{2,1,0:T(8,128)(2,1)} %slab_hbm.1, s32[8]{0:T(128)} %counts.1, s32[3,8]{1,0:T(4,128)} %select_select_fusion.table), custom_call_target="tpu_custom_call" | custom-call | flops 11000000512 | bytes 7000000 | tf_op jit(solution)/shard_map/pallas_call | solution.py:383
  72.4 1.6 %copy.8 = bf16[512,128]{1,0:T(8,128)(2,1)} copy(bf16[512,128]{1,0:T(8,128)(2,1)} %bitcast.5) | data formatting | bytes 262144
  (3 shorter events, 0.0 us)

commit v5 on v4

--- a/solution.py
+++ b/solution.py
@@ -218,11 +218,11 @@
         )
 
     def kinds(dys):
-        return [(dy, zt) for dy in dys for zt in range(3) if dy > 1 or zt > 0]
+        return [(dy, zt) for zt in (1, 2, 0) for dy in dys if dy > 1 or zt > 0]
 
     def dress(r, carry):
         cs = pl.ds(r * per, per)
-        for dys in ((2, 3), (0, 1)):
+        for dys in ((0, 2), (1, 3)):
             blocks = [(dz, dy) for dy in dys for dz in range(2)]
             tables = []
             for dz, dy in blocks:

time: 74.1 us -> 73.1 us (0.987)
  Pallas kernels: 71 us -> 70 us
    pallas_call x1, Pallas kernels: 71 us -> 70 us  [body(): pl.pallas_call(kernel, out_shape=jax.ShapeDtypeStruct((2, 4, 2, 32, 128),...]
where the time goes in v5:
time: 73.1 us; the launch traced here: 72.9 us
  Pallas kernels  70 us (96%)
  local copies, waits for them, and re-layouts  1.57 us (2%)
    pallas_call x1, Pallas kernels, body(): pl.pallas_call(kernel, out_shape=jax.ShapeDtypeStruct((2, 4, 2, 32, 128),...  70 us
    unnamed x1, local copies, waits for them, and re-layouts  1.57 us

profile of v5, /device:TPU:1, one launch (start us, length us, event | category | flops | bytes accessed | tf_op | source)
XLA Modules:
  0.0 72.9 jit_solution(1845889485468828383)
XLA Ops:
  0.7 0.7 select_select_fusion.table
  1.3 70.0 %shard_map.55 = bf16[2,4,2,32,128]{4,3,2,1,0:T(8,128)(2,1)} custom-call(bf16[32,32,2048]{2,1,0:T(8,128)(2,1)} %amp_hbm.1, bf16[16,2048]{1,0:T(8,128)(2,1)} %bitcast.6, bf16[32,256,128]{2,1,0:T(8,128)(2,1)} %slab_hbm.1, s32[8]{0:T(128)} %counts.1, s32[3,8]{1,0:T(4,128)} %select_select_fusion.table), custom_call_target="tpu_custom_call" | custom-call | flops 11000000512 | bytes 7000000 | tf_op jit(solution)/shard_map/pallas_call | solution.py:383
  71.3 1.6 %copy.8 = bf16[512,128]{1,0:T(8,128)(2,1)} copy(bf16[512,128]{1,0:T(8,128)(2,1)} %bitcast.5) | data formatting | bytes 262144
  (3 shorter events, 0.0 us)

commit v6 on v5

--- a/solution.py
+++ b/solution.py
@@ -139,7 +139,7 @@
         at[d1] = (at[d1] + source) % 4
         ref = gs[p].at[at["z"] // 2, at["x"], at["z"] % 2, at["y"], core]
         return pltpu.make_async_remote_copy(
-            src_ref=ref, dst_ref=ref,
+            src_ref=cyc_hbm.at[:, pl.ds(sum(WIDTHS[:p]), WIDTHS[p])], dst_ref=ref,
             send_sem=gather_send.at[p, step - 1], recv_sem=gather_recv.at[p, step - 1],
             device_id=neighbour(d1, step), device_id_type=MESH,
         )
@@ -170,9 +170,10 @@
         )
 
     for p in range(3):
-        load_cyc[p].wait()
         for step in steps:
             go(first(p, step, 0))
+    for copy in load_cyc:
+        copy.wait()
     load_amp.wait()
     transpose_blocks(0, 1)
     for p in range(3):
@@ -190,14 +191,23 @@
             spread(p, slot + 1)
     go(slab_fetch(quarter[0], 0))
     transpose_blocks(3, 8)
-    for sub in range(4):
+    for sub in range(3):
         for p in range(3):
             for slot in range(3):
                 along_third(p, sub, slot + 1, slot).wait_recv()
             go(to_sibling(p, seconds[p][sub], ALL, sub, core))
+            if sub == 0:
+                go(to_sibling(p, seconds[p][3], thirds[p][0], 3, core))
+    for slot in range(3):
+        for p in range(3):
+            along_third(p, 3, slot + 1, slot).wait_recv()
+            go(to_sibling(p, seconds[p][3], thirds[p][slot + 1], 4 + slot, core))
     for p in range(3):
-        for sub in range(4):
+        for sub in range(3):
             to_sibling(p, seconds[p][sub], ALL, sub, 1 - core).wait_recv()
+        for i in range(4):
+            to_sibling(p, seconds[p][3], thirds[p][i], 3 + i, 1 - core).wait_recv()
+
     per = 32 // NR
     spots = ((0, 0), (1, 0), (1, 1), (0, 1))
     y_of = (y, y, (y + 1) % 4, (y + 3) % 4)
@@ -310,6 +320,16 @@
     for slot, q in ((6, 0), (7, 3), (8, 1), (9, 2)):
         slab_piece((1, 1), quarter[q], 8, 1 - core, slot, sibling).wait_recv()
     lax.fori_loop(0, NR - 1, ladder_second, 0)
+
+    def drain(r, carry):
+        for dy, zt in kinds(range(4)):
+            message(r, dy, zt).wait_send()
+        return carry
+
+    for copy in sent:
+        copy.wait_send()
+    lax.fori_loop(0, NR - 1, drain, 0)
+
     def home(which, place, side):
         at = device(x, (y + which) % 4, (z + 2 * place) % 4, side)
         land = (near, beyond)[place].at[which, core]
@@ -336,15 +356,7 @@
                     home(which, place, side).start()
     near[0, core] = result[0, core, :, 0:48]
 
-    for copy in sent:
-        copy.wait_send()
-
-    def drain(r, carry):
-        for dy, zt in kinds(range(4)):
-            message(r, dy, zt).wait_send()
-        return carry
-
-    lax.fori_loop(0, NR, drain, 0)
+    drain(NR - 1, 0)
 
     def arrival(which, place, side):
         land = (near, beyond)[place].at[which, side]
@@ -402,8 +414,8 @@
             dma((5,)),
             dma((3, 18)),
             dma((3, 18)),
-            dma((3, 4)),
-            dma((3, 4)),
+            dma((3, 7)),
+            dma((3, 7)),
             dma((NR, 4, 3)),
             dma((NR, 4, 3)),
             dma((10,)),

time: 73.1 us -> 72.5 us (level)
  no operation moved by 1% of the time
where the time goes in v6:
time: 72.5 us; the launch traced here: 72.3 us
  Pallas kernels  69.4 us (96%)
  local copies, waits for them, and re-layouts  1.57 us (2%)
    pallas_call x1, Pallas kernels, body(): pl.pallas_call(kernel, out_shape=jax.ShapeDtypeStruct((2, 4, 2, 32, 128),...  69.4 us
    unnamed x1, local copies, waits for them, and re-layouts  1.57 us

profile of v6, /device:TPU:1, one launch (start us, length us, event | category | flops | bytes accessed | tf_op | source)
XLA Modules:
  0.0 72.3 jit_solution(816215155500150508)
XLA Ops:
  0.7 0.7 select_select_fusion.table
  1.3 69.4 %shard_map.55 = bf16[2,4,2,32,128]{4,3,2,1,0:T(8,128)(2,1)} custom-call(bf16[32,32,2048]{2,1,0:T(8,128)(2,1)} %amp_hbm.1, bf16[16,2048]{1,0:T(8,128)(2,1)} %bitcast.6, bf16[32,256,128]{2,1,0:T(8,128)(2,1)} %slab_hbm.1, s32[8]{0:T(128)} %counts.1, s32[3,8]{1,0:T(4,128)} %select_select_fusion.table), custom_call_target="tpu_custom_call" | custom-call | flops 11000000512 | bytes 7000000 | tf_op jit(solution)/shard_map/pallas_call | solution.py:395
  70.8 1.6 %copy.8 = bf16[512,128]{1,0:T(8,128)(2,1)} copy(bf16[512,128]{1,0:T(8,128)(2,1)} %bitcast.5) | data formatting | bytes 262144
  (3 shorter events, 0.0 us)

commit v7 on v6

--- a/solution.py
+++ b/solution.py
@@ -174,8 +174,6 @@
             go(first(p, step, 0))
     for copy in load_cyc:
         copy.wait()
-    load_amp.wait()
-    transpose_blocks(0, 1)
     for p in range(3):
         for step in steps:
             first(p, step, 4 - step).wait_recv()
@@ -184,7 +182,8 @@
         spread(p, 0)
     load_slab.wait()
     go(slab_piece((0, 0), 0, 32, core, 1, sibling))
-    transpose_blocks(1, 3)
+    load_amp.wait()
+    transpose_blocks(0, 3)
     for slot in range(3):
         for p in range(3):
             along_second(p, slot + 1, slot).wait_recv()

time: 72.5 us -> 72.5 us (level)
  no operation moved by 1% of the time
where the time goes in v7:
time: 72.5 us; the launch traced here: 72.3 us
  Pallas kernels  69.4 us (96%)
  local copies, waits for them, and re-layouts  1.57 us (2%)
    pallas_call x1, Pallas kernels, body(): pl.pallas_call(kernel, out_shape=jax.ShapeDtypeStruct((2, 4, 2, 32, 128),...  69.4 us
    unnamed x1, local copies, waits for them, and re-layouts  1.57 us

profile of v7, /device:TPU:1, one launch (start us, length us, event | category | flops | bytes accessed | tf_op | source)
XLA Modules:
  0.0 72.3 jit_solution(15436957327543730045)
XLA Ops:
  0.7 0.7 select_select_fusion.table
  1.3 69.4 %shard_map.55 = bf16[2,4,2,32,128]{4,3,2,1,0:T(8,128)(2,1)} custom-call(bf16[32,32,2048]{2,1,0:T(8,128)(2,1)} %amp_hbm.1, bf16[16,2048]{1,0:T(8,128)(2,1)} %bitcast.6, bf16[32,256,128]{2,1,0:T(8,128)(2,1)} %slab_hbm.1, s32[8]{0:T(128)} %counts.1, s32[3,8]{1,0:T(4,128)} %select_select_fusion.table), custom_call_target="tpu_custom_call" | custom-call | flops 11000000512 | bytes 7000000 | tf_op jit(solution)/shard_map/pallas_call | solution.py:394
  70.8 1.6 %copy.8 = bf16[512,128]{1,0:T(8,128)(2,1)} copy(bf16[512,128]{1,0:T(8,128)(2,1)} %bitcast.5) | data formatting | bytes 262144
  (3 shorter events, 0.0 us)
